TPU v7x, 128 devices: a whole 4x4x4 slice. The times are simulated.
128 devices in a mesh: dp: 128 (over y, x, z, core).
Axes of the slice: x: 4, y: 4, z: 4, core: 2. Of those that a mesh axis runs over, the one named last changes fastest.
Arguments:
- img_emb: bfloat16 [65536, 1152], P('dp'), may hold values from -6 to 6
- txt_emb: bfloat16 [65536, 1152], P('dp'), may hold values from -6 to 6
- img_proj: bfloat16 [1152, 1152], replicated, may hold values from -0.1875 to 0.1875
- txt_proj: bfloat16 [1152, 1152], replicated, may hold values from -0.1875 to 0.1875
- log_scale: float32 [1], replicated, may hold values from 1.1 to 2.1
- bias: float32 [1], replicated, may hold values from -3 to -1
Outputs:
- d_img_emb: bfloat16 [65536, 1152], P('dp')
- d_txt_emb: bfloat16 [65536, 1152], P('dp')
- d_img_proj: float32 [1152, 1152], replicated
- d_txt_proj: float32 [1152, 1152], replicated
All inputs are finite; a program needn't handle non-finite values.
Results may differ from a plain program's by a relative error of at most 0.02.
Values may be sent and summed in bfloat16 or wider, within the bound.
A program may use at most 128 MiB of HBM per device.

v0:
```python
import jax
import jax.numpy as jnp
from jax import lax
from jax.sharding import PartitionSpec as P

REACH = 3


def from_behind(shard, axis, by):
    size = lax.axis_size(axis)
    return lax.ppermute(shard, axis, [(i, (i + by) % size) for i in range(size)])


def unit_rows(embeddings, projection):
    projected = jnp.dot(embeddings, projection, preferred_element_type=jnp.float32)
    row_norm = jnp.sqrt(jnp.sum(projected * projected, axis=1, keepdims=True) + 1e-06)
    return (projected / row_norm, row_norm)


def unit_back(grad_unit, unit_vals, row_norm):
    inner = jnp.sum(unit_vals * grad_unit, axis=1, keepdims=True)
    return (grad_unit - unit_vals * inner) / row_norm


def pair_grads(image_block, text_block, logit_scale, logit_bias, own_block):
    logits = (
        logit_scale * jnp.dot(image_block, text_block.T, preferred_element_type=jnp.float32)
        + logit_bias
    )
    coefficients = jax.nn.sigmoid(logits)
    if own_block:
        count = logits.shape[0]
        diagonal_mask = jnp.arange(count)[:, None] == jnp.arange(count)[None, :]
        coefficients = jnp.where(diagonal_mask, coefficients - 1.0, coefficients)
    coefficients = coefficients.astype(jnp.bfloat16)
    image_term = logit_scale * jnp.dot(coefficients, text_block, preferred_element_type=jnp.float32)
    text_term = logit_scale * jnp.dot(
        coefficients.T, image_block, preferred_element_type=jnp.float32
    )
    return (image_term, text_term)


def advance(visitor, step_by):
    return from_behind(visitor, "dp", step_by)


def travel(image_block, visitor, step_by, offsets, hop_first, logit_scale, logit_bias):
    image_total = jnp.zeros(image_block.shape, jnp.float32)
    carried = None
    for position, reach_step in enumerate(offsets):
        if position > 0 or hop_first:
            visitor = advance(visitor, step_by)
        if carried is not None:
            carried = from_behind(carried.astype(jnp.bfloat16), "dp", step_by).astype(carried.dtype)
        image_term, text_term = pair_grads(
            image_block, visitor, logit_scale, logit_bias, reach_step == 0
        )
        image_total = image_total + image_term
        carried = text_term if carried is None else carried + text_term
    final_offset = offsets[-1]
    carried = from_behind(carried.astype(jnp.bfloat16), "dp", final_offset).astype(carried.dtype)
    return (image_total, carried)


def body(img_emb, txt_emb, img_proj, txt_proj, log_scale, bias):
    logit_scale = jnp.exp(log_scale[0])
    logit_bias = bias[0]
    img_unit, img_norm = unit_rows(img_emb, img_proj)
    txt_unit, txt_norm = unit_rows(txt_emb, txt_proj)
    img_z = img_unit.astype(jnp.bfloat16)
    txt_z = txt_unit.astype(jnp.bfloat16)
    jumped = from_behind(txt_z, "dp", -REACH)
    journeys = (jumped, 1, list(range(REACH, -REACH - 1, -1)), False)
    visitor, step_by, offsets, hop_first = journeys
    image_part, text_part = travel(
        img_z, visitor, step_by, offsets, hop_first, logit_scale, logit_bias
    )
    img_du = unit_back(image_part, img_unit, img_norm).astype(jnp.bfloat16)
    txt_du = unit_back(text_part, txt_unit, txt_norm).astype(jnp.bfloat16)
    d_img_emb = jnp.dot(img_du, img_proj.T, preferred_element_type=jnp.float32).astype(jnp.bfloat16)
    d_txt_emb = jnp.dot(txt_du, txt_proj.T, preferred_element_type=jnp.float32).astype(jnp.bfloat16)
    img_weight_terms = jnp.dot(img_emb.T, img_du, preferred_element_type=jnp.float32)
    txt_weight_terms = jnp.dot(txt_emb.T, txt_du, preferred_element_type=jnp.float32)
    d_img_proj, d_txt_proj = lax.psum((img_weight_terms, txt_weight_terms), "dp")
    return (d_img_emb, d_txt_emb, d_img_proj, d_txt_proj)


def solution(mesh):
    return jax.shard_map(
        body,
        mesh=mesh,
        in_specs=(P("dp", None), P("dp", None), P(), P(), P(), P()),
        out_specs=(P("dp", None), P("dp", None), P(), P()),
        check_vma=False,
    )
```

profile of v0, /device:TPU:1, one launch (start us, length us, event | category | flops | bytes accessed | tf_op | source)
XLA Modules:
  0.0 434.1 jit_solution(6529750671480559017)
XLA Ops:
  7.2 4.2 multiply_reduce_fusion.1
  11.4 0.3 fusion.48
  11.7 9.9 %collective-permute-start = (bf16[512,1152]{1,0:T(8,128)(2,1)S(1)}, bf16[512,1152]{1,0:T(8,128)(2,1)S(1)}, u32[]{:S(2)}, u32[]{:S(2)}) collective-permute-start(bf16[512,1152]{1,0:T(8,128)(2,1)S(1)} %fusion.48), channel_id=1, source_target_pairs={{0,125},{1,126},{2,127},{3,0},{4,1},{5,2},{6,3},{7,4},{8,5},{9,6},... | collective-permute-start | bytes 3538952 | tf_op jit(solution)/shard_map/ppermute | solution.py:11
  22.9 2.0 multiply_reduce_fusion.2
  24.9 0.3 fusion.47
  25.2 22.9 %collective-permute-done = bf16[512,1152]{1,0:T(8,128)(2,1)S(1)} collective-permute-done((bf16[512,1152]{1,0:T(8,128)(2,1)S(1)}, bf16[512,1152]{1,0:T(8,128)(2,1)S(1)}, u32[]{:S(2)}, u32[]{:S(2)}) %collective-permute-start) | collective-permute-done | bytes 1179680 | tf_op jit(solution)/shard_map/ppermute | solution.py:11
  48.1 1.0 fusion.45
  49.1 0.9 fusion.1
  50.1 11.2 %collective-permute-done.1 = bf16[512,1152]{1,0:T(8,128)(2,1)S(1)} collective-permute-done((bf16[512,1152]{1,0:T(8,128)(2,1)S(1)}, bf16[512,1152]{1,0:T(8,128)(2,1)S(1)}, u32[]{:S(2)}, u32[]{:S(2)}) %collective-permute-start.1) | collective-permute-done | bytes 1179680 | tf_op jit(solution)/shard_map/ppermute | solution.py:11
  61.2 2.5 collective-permute-start.2
  63.7 1.0 fusion.44
  64.7 9.1 %collective-permute-done.7 = bf16[512,1152]{1,0:T(8,128)(2,1)S(1)} collective-permute-done((bf16[512,1152]{1,0:T(8,128)(2,1)S(1)}, bf16[512,1152]{1,0:T(8,128)(2,1)S(1)}, u32[]{:S(2)}, u32[]{:S(2)}) %collective-permute-start.7) | collective-permute-done | bytes 1179680 | tf_op jit(solution)/shard_map/ppermute | solution.py:11
  73.9 0.9 add_convert_fusion.5
  74.8 2.5 collective-permute-start.8
  77.3 9.2 %collective-permute-done.2 = bf16[512,1152]{1,0:T(8,128)(2,1)S(1)} collective-permute-done((bf16[512,1152]{1,0:T(8,128)(2,1)S(1)}, bf16[512,1152]{1,0:T(8,128)(2,1)S(1)}, u32[]{:S(2)}, u32[]{:S(2)}) %collective-permute-start.2) | collective-permute-done | bytes 1179680 | tf_op jit(solution)/shard_map/ppermute | solution.py:11
  86.5 2.5 collective-permute-start.3
  89.0 1.0 fusion.43
  90.0 0.9 convolution_multiply_fusion.4
  90.9 8.2 %collective-permute-done.8 = bf16[512,1152]{1,0:T(8,128)(2,1)S(1)} collective-permute-done((bf16[512,1152]{1,0:T(8,128)(2,1)S(1)}, bf16[512,1152]{1,0:T(8,128)(2,1)S(1)}, u32[]{:S(2)}, u32[]{:S(2)}) %collective-permute-start.8) | collective-permute-done | bytes 1179680 | tf_op jit(solution)/shard_map/ppermute | solution.py:11
  99.4 2.5 collective-permute-start.9
  101.9 9.9 %collective-permute-done.3 = bf16[512,1152]{1,0:T(8,128)(2,1)S(1)} collective-permute-done((bf16[512,1152]{1,0:T(8,128)(2,1)S(1)}, bf16[512,1152]{1,0:T(8,128)(2,1)S(1)}, u32[]{:S(2)}, u32[]{:S(2)}) %collective-permute-start.3) | collective-permute-done | bytes 1179680 | tf_op jit(solution)/shard_map/ppermute | solution.py:11
  111.8 2.5 collective-permute-start.4
  114.3 1.0 fusion.46
  115.3 0.9 convolution_multiply_fusion.3
  116.2 8.2 %collective-permute-done.9 = bf16[512,1152]{1,0:T(8,128)(2,1)S(1)} collective-permute-done((bf16[512,1152]{1,0:T(8,128)(2,1)S(1)}, bf16[512,1152]{1,0:T(8,128)(2,1)S(1)}, u32[]{:S(2)}, u32[]{:S(2)}) %collective-permute-start.9) | collective-permute-done | bytes 1179680 | tf_op jit(solution)/shard_map/ppermute | solution.py:11
  124.4 0.2 add_convert_fusion.3
  124.7 2.5 collective-permute-start.10
  127.2 0.9 fusion.49
  128.1 0.9 convolution_add_fusion.5
  128.9 8.2 %collective-permute-done.4 = bf16[512,1152]{1,0:T(8,128)(2,1)S(1)} collective-permute-done((bf16[512,1152]{1,0:T(8,128)(2,1)S(1)}, bf16[512,1152]{1,0:T(8,128)(2,1)S(1)}, u32[]{:S(2)}, u32[]{:S(2)}) %collective-permute-start.4) | collective-permute-done | bytes 1179680 | tf_op jit(solution)/shard_map/ppermute | solution.py:11
  137.1 2.5 collective-permute-start.5
  139.6 1.0 fusion.42
  140.6 0.9 convolution_multiply_fusion.2
  141.5 8.2 %collective-permute-done.10 = bf16[512,1152]{1,0:T(8,128)(2,1)S(1)} collective-permute-done((bf16[512,1152]{1,0:T(8,128)(2,1)S(1)}, bf16[512,1152]{1,0:T(8,128)(2,1)S(1)}, u32[]{:S(2)}, u32[]{:S(2)}) %collective-permute-start.10) | collective-permute-done | bytes 1179680 | tf_op jit(solution)/shard_map/ppermute | solution.py:11
  149.7 0.2 add_convert_fusion.2
  149.9 2.5 collective-permute-start.11
  152.5 0.9 convolution_add_fusion.4
  153.4 0.9 convolution_add_fusion.3
  154.3 8.1 %collective-permute-done.5 = bf16[512,1152]{1,0:T(8,128)(2,1)S(1)} collective-permute-done((bf16[512,1152]{1,0:T(8,128)(2,1)S(1)}, bf16[512,1152]{1,0:T(8,128)(2,1)S(1)}, u32[]{:S(2)}, u32[]{:S(2)}) %collective-permute-start.5) | collective-permute-done | bytes 1179680 | tf_op jit(solution)/shard_map/ppermute | solution.py:11
  162.4 2.5 collective-permute-start.6
  164.8 1.0 fusion.41
  165.9 0.9 convolution_multiply_fusion.1
  166.7 8.2 %collective-permute-done.11 = bf16[512,1152]{1,0:T(8,128)(2,1)S(1)} collective-permute-done((bf16[512,1152]{1,0:T(8,128)(2,1)S(1)}, bf16[512,1152]{1,0:T(8,128)(2,1)S(1)}, u32[]{:S(2)}, u32[]{:S(2)}) %collective-permute-start.11) | collective-permute-done | bytes 1179680 | tf_op jit(solution)/shard_map/ppermute | solution.py:11
  175.2 2.8 collective-permute-start.12
  178.0 0.9 convolution_add_fusion.2
  178.9 0.9 convolution_add_fusion.1
  179.8 7.9 %collective-permute-done.6 = bf16[512,1152]{1,0:T(8,128)(2,1)S(1)} collective-permute-done((bf16[512,1152]{1,0:T(8,128)(2,1)S(1)}, bf16[512,1152]{1,0:T(8,128)(2,1)S(1)}, u32[]{:S(2)}, u32[]{:S(2)}) %collective-permute-start.6) | collective-permute-done | bytes 1179680 | tf_op jit(solution)/shard_map/ppermute | solution.py:11
  187.6 1.0 fusion.40
  188.7 0.9 convolution_multiply_fusion
  189.5 10.7 %collective-permute-done.12 = bf16[512,1152]{1,0:T(8,128)(2,1)S(1)} collective-permute-done((bf16[512,1152]{1,0:T(8,128)(2,1)S(1)}, bf16[512,1152]{1,0:T(8,128)(2,1)S(1)}, u32[]{:S(2)}, u32[]{:S(2)}) %collective-permute-start.12) | collective-permute-done | bytes 1179680 | tf_op jit(solution)/shard_map/ppermute | solution.py:11
  200.5 12.9 %collective-permute-start.13 = (bf16[512,1152]{1,0:T(8,128)(2,1)S(1)}, bf16[512,1152]{1,0:T(8,128)(2,1)S(1)}, u32[]{:S(2)}, u32[]{:S(2)}) collective-permute-start(bf16[512,1152]{1,0:T(8,128)(2,1)S(1)} %add_convert_fusion), channel_id=1, source_target_pairs={{0,125},{1,126},{2,127},{3,0},{4,1},{5,2},{6,3},{7,4},{8,5},{9,6},... | collective-permute-start | bytes 3538952 | tf_op jit(solution)/shard_map/ppermute | solution.py:11
  213.4 1.2 multiply_reduce_fusion
  214.6 0.4 divide_convert_fusion
  215.0 4.1 convolution_bitcast_fusion.1
  219.2 19.5 %collective-permute-done.13 = bf16[512,1152]{1,0:T(8,128)(2,1)S(1)} collective-permute-done((bf16[512,1152]{1,0:T(8,128)(2,1)S(1)}, bf16[512,1152]{1,0:T(8,128)(2,1)S(1)}, u32[]{:S(2)}, u32[]{:S(2)}) %collective-permute-start.13) | collective-permute-done | bytes 1179680 | tf_op jit(solution)/shard_map/ppermute | solution.py:11
  238.6 0.5 fusion.2
  239.1 0.5 fusion.4
  239.6 1.0 copy-done.2
  240.7 4.1 convolution_bitcast_fusion
  244.8 4.3 convolution_convert_fusion.1
  249.1 2.9 convolution_convert_fusion
  252.0 161.6 %all-reduce.3.cloned.1.call-done = (f32[1152,1152]{0,1:T(8,128)}, f32[1152,1152]{0,1:T(8,128)}) async-done(((f32[1152,1152]{0,1:T(8,128)}, f32[1152,1152]{0,1:T(8,128)}), (f32[1152,1152]{0,1:T(8,128)}, f32[1152,1152]{0,1:T(8,128)})) %all-reduce.3.cloned.1.call-update) | async-done | bytes 10616848 | tf_op jit(solution)/shard_map/psum | solution.py:84
  413.6 6.9 %copy.10 = f32[1152,1152]{1,0:T(8,128)} copy(f32[1152,1152]{0,1:T(8,128)} %get-tuple-element.8) | data formatting | bytes 10616832
  420.4 6.9 %copy.11 = f32[1152,1152]{1,0:T(8,128)} copy(f32[1152,1152]{0,1:T(8,128)} %get-tuple-element.9) | data formatting | bytes 10616832
  (22 shorter events, 0.8 us)
Async XLA Ops:
  7.2 15.8 %copy-start = (bf16[1152,1152]{1,0:T(8,128)(2,1)S(1)}, bf16[1152,1152]{1,0:T(8,128)(2,1)}, u32[]{:S(2)}) copy-start(bf16[1152,1152]{1,0:T(8,128)(2,1)} %param.8) | copy-start | bytes 7962628
  7.2 406.4 %all-reduce.3.cloned.1.call-start = ((), (), s32[]{:S(2)}) async-start(), calls=%async_computation | async-start | bytes 21233664 | tf_op jit(solution)/shard_map/psum | solution.py:84
  11.4 11.5 %copy-start.4 = (bf16[512,1152]{1,0:T(8,128)(2,1)S(1)}, bf16[512,1152]{1,0:T(8,128)(2,1)}, u32[]{:S(2)}) copy-start(bf16[512,1152]{1,0:T(8,128)(2,1)} %param.6) | copy-start | bytes 3538948
  11.7 36.4 %collective-permute-start = (bf16[512,1152]{1,0:T(8,128)(2,1)S(1)}, bf16[512,1152]{1,0:T(8,128)(2,1)S(1)}, u32[]{:S(2)}, u32[]{:S(2)}) collective-permute-start(bf16[512,1152]{1,0:T(8,128)(2,1)S(1)} %fusion.48), channel_id=1, source_target_pairs={{0,125},{1,126},{2,127},{3,0},{4,1},{5,2},{6,3},{7,4},{8,5},{9,6},... | collective-permute-start | bytes 3538952 | tf_op jit(solution)/shard_map/ppermute | solution.py:11
  48.1 13.2 %collective-permute-start.1 = (bf16[512,1152]{1,0:T(8,128)(2,1)S(1)}, bf16[512,1152]{1,0:T(8,128)(2,1)S(1)}, u32[]{:S(2)}, u32[]{:S(2)}) collective-permute-start(bf16[512,1152]{1,0:T(8,128)(2,1)S(1)} %collective-permute-done), channel_id=1, source_target_pairs={{0,1},{1,2},{2,3},{3,4},{4,5},{5,6},{6,7},{7,8},{8,9},{9,10},{10,1... | collective-permute-start | bytes 3538952 | tf_op jit(solution)/shard_map/ppermute | solution.py:11
  50.0 23.9 %collective-permute-start.7 = (bf16[512,1152]{1,0:T(8,128)(2,1)S(1)}, bf16[512,1152]{1,0:T(8,128)(2,1)S(1)}, u32[]{:S(2)}, u32[]{:S(2)}) collective-permute-start(bf16[512,1152]{1,0:T(8,128)(2,1)S(1)} %fusion.1), channel_id=1, source_target_pairs={{0,1},{1,2},{2,3},{3,4},{4,5},{5,6},{6,7},{7,8},{8,9},{9,10},{10,1... | collective-permute-start | bytes 3538952 | tf_op jit(solution)/shard_map/ppermute | solution.py:11
  61.2 25.3 %collective-permute-start.2 = (bf16[512,1152]{1,0:T(8,128)(2,1)S(1)}, bf16[512,1152]{1,0:T(8,128)(2,1)S(1)}, u32[]{:S(2)}, u32[]{:S(2)}) collective-permute-start(bf16[512,1152]{1,0:T(8,128)(2,1)S(1)} %collective-permute-done.1), channel_id=1, source_target_pairs={{0,1},{1,2},{2,3},{3,4},{4,5},{5,6},{6,7},{7,8},{8,9},{9,10},{10,1... | collective-permute-start | bytes 3538952 | tf_op jit(solution)/shard_map/ppermute | solution.py:11
  74.8 24.4 %collective-permute-start.8 = (bf16[512,1152]{1,0:T(8,128)(2,1)S(1)}, bf16[512,1152]{1,0:T(8,128)(2,1)S(1)}, u32[]{:S(2)}, u32[]{:S(2)}) collective-permute-start(bf16[512,1152]{1,0:T(8,128)(2,1)S(1)} %add_convert_fusion.5), channel_id=1, source_target_pairs={{0,1},{1,2},{2,3},{3,4},{4,5},{5,6},{6,7},{7,8},{8,9},{9,10},{10,1... | collective-permute-start | bytes 3538952 | tf_op jit(solution)/shard_map/ppermute | solution.py:11
  86.5 25.3 %collective-permute-start.3 = (bf16[512,1152]{1,0:T(8,128)(2,1)S(1)}, bf16[512,1152]{1,0:T(8,128)(2,1)S(1)}, u32[]{:S(2)}, u32[]{:S(2)}) collective-permute-start(bf16[512,1152]{1,0:T(8,128)(2,1)S(1)} %collective-permute-done.2), channel_id=1, source_target_pairs={{0,1},{1,2},{2,3},{3,4},{4,5},{5,6},{6,7},{7,8},{8,9},{9,10},{10,1... | collective-permute-start | bytes 3538952 | tf_op jit(solution)/shard_map/ppermute | solution.py:11
  99.4 25.1 %collective-permute-start.9 = (bf16[512,1152]{1,0:T(8,128)(2,1)S(1)}, bf16[512,1152]{1,0:T(8,128)(2,1)S(1)}, u32[]{:S(2)}, u32[]{:S(2)}) collective-permute-start(bf16[512,1152]{1,0:T(8,128)(2,1)S(1)} %add_convert_fusion.4), channel_id=1, source_target_pairs={{0,1},{1,2},{2,3},{3,4},{4,5},{5,6},{6,7},{7,8},{8,9},{9,10},{10,1... | collective-permute-start | bytes 3538952 | tf_op jit(solution)/shard_map/ppermute | solution.py:11
  111.8 25.3 %collective-permute-start.4 = (bf16[512,1152]{1,0:T(8,128)(2,1)S(1)}, bf16[512,1152]{1,0:T(8,128)(2,1)S(1)}, u32[]{:S(2)}, u32[]{:S(2)}) collective-permute-start(bf16[512,1152]{1,0:T(8,128)(2,1)S(1)} %collective-permute-done.3), channel_id=1, source_target_pairs={{0,1},{1,2},{2,3},{3,4},{4,5},{5,6},{6,7},{7,8},{8,9},{9,10},{10,1... | collective-permute-start | bytes 3538952 | tf_op jit(solution)/shard_map/ppermute | solution.py:11
  124.7 25.1 %collective-permute-start.10 = (bf16[512,1152]{1,0:T(8,128)(2,1)S(1)}, bf16[512,1152]{1,0:T(8,128)(2,1)S(1)}, u32[]{:S(2)}, u32[]{:S(2)}) collective-permute-start(bf16[512,1152]{1,0:T(8,128)(2,1)S(1)} %add_convert_fusion.3), channel_id=1, source_target_pairs={{0,1},{1,2},{2,3},{3,4},{4,5},{5,6},{6,7},{7,8},{8,9},{9,10},{10,1... | collective-permute-start | bytes 3538952 | tf_op jit(solution)/shard_map/ppermute | solution.py:11
  137.1 25.3 %collective-permute-start.5 = (bf16[512,1152]{1,0:T(8,128)(2,1)S(1)}, bf16[512,1152]{1,0:T(8,128)(2,1)S(1)}, u32[]{:S(2)}, u32[]{:S(2)}) collective-permute-start(bf16[512,1152]{1,0:T(8,128)(2,1)S(1)} %collective-permute-done.4), channel_id=1, source_target_pairs={{0,1},{1,2},{2,3},{3,4},{4,5},{5,6},{6,7},{7,8},{8,9},{9,10},{10,1... | collective-permute-start | bytes 3538952 | tf_op jit(solution)/shard_map/ppermute | solution.py:11
  149.9 25.1 %collective-permute-start.11 = (bf16[512,1152]{1,0:T(8,128)(2,1)S(1)}, bf16[512,1152]{1,0:T(8,128)(2,1)S(1)}, u32[]{:S(2)}, u32[]{:S(2)}) collective-permute-start(bf16[512,1152]{1,0:T(8,128)(2,1)S(1)} %add_convert_fusion.2), channel_id=1, source_target_pairs={{0,1},{1,2},{2,3},{3,4},{4,5},{5,6},{6,7},{7,8},{8,9},{9,10},{10,1... | collective-permute-start | bytes 3538952 | tf_op jit(solution)/shard_map/ppermute | solution.py:11
  162.4 25.3 %collective-permute-start.6 = (bf16[512,1152]{1,0:T(8,128)(2,1)S(1)}, bf16[512,1152]{1,0:T(8,128)(2,1)S(1)}, u32[]{:S(2)}, u32[]{:S(2)}) collective-permute-start(bf16[512,1152]{1,0:T(8,128)(2,1)S(1)} %collective-permute-done.5), channel_id=1, source_target_pairs={{0,1},{1,2},{2,3},{3,4},{4,5},{5,6},{6,7},{7,8},{8,9},{9,10},{10,1... | collective-permute-start | bytes 3538952 | tf_op jit(solution)/shard_map/ppermute | solution.py:11
  175.2 25.1 %collective-permute-start.12 = (bf16[512,1152]{1,0:T(8,128)(2,1)S(1)}, bf16[512,1152]{1,0:T(8,128)(2,1)S(1)}, u32[]{:S(2)}, u32[]{:S(2)}) collective-permute-start(bf16[512,1152]{1,0:T(8,128)(2,1)S(1)} %add_convert_fusion.1), channel_id=1, source_target_pairs={{0,1},{1,2},{2,3},{3,4},{4,5},{5,6},{6,7},{7,8},{8,9},{9,10},{10,1... | collective-permute-start | bytes 3538952 | tf_op jit(solution)/shard_map/ppermute | solution.py:11
  200.5 38.1 %collective-permute-start.13 = (bf16[512,1152]{1,0:T(8,128)(2,1)S(1)}, bf16[512,1152]{1,0:T(8,128)(2,1)S(1)}, u32[]{:S(2)}, u32[]{:S(2)}) collective-permute-start(bf16[512,1152]{1,0:T(8,128)(2,1)S(1)} %add_convert_fusion), channel_id=1, source_target_pairs={{0,125},{1,126},{2,127},{3,0},{4,1},{5,2},{6,3},{7,4},{8,5},{9,6},... | collective-permute-start | bytes 3538952 | tf_op jit(solution)/shard_map/ppermute | solution.py:11
  215.0 4.1 copy-start.1
  239.1 1.6 copy-start.5
  239.6 1.0 copy-start.2
  244.8 4.3 copy-start.3
  244.8 4.3 copy-start.6
Sparse Core Ops, SparseCore 0:
  244.9 168.6 all-reduce.2
where the time goes:
time: 435 us; the launch traced here: 434 us
  waiting for transfers between devices  311 us (71%)
  starting transfers between devices  48.2 us (11%)
  matrix products  41.3 us (9%)
  between operations  15.7 us (4%)
  local copies, waits for them, and re-layouts  14.8 us (3%)
    psum x1, waiting for transfers between devices, body(): lax.psum((img_weight_terms, txt_weight_terms), 'dp')  162 us
    ppermute x14, waiting for transfers between devices, from_behind(): lax.ppermute(shard, axis, [(i, (i + by) % size) for i in range(size)])  150 us
    ppermute x14, starting transfers between devices, from_behind(): lax.ppermute(shard, axis, [(i, (i + by) % size) for i in range(size)])  48.2 us
    unnamed x16, local copies, waits for them, and re-layouts  14.8 us
  transfers between devices with their start and end apart: 15, of which 15 were waited for; matrix products, arithmetic and copies ran while one was open for 8% of the time, Pallas kernels for 0%

commit v1 on v0

v1 whole, which is shorter than its diff:
```python
import functools

import jax
import jax.numpy as jnp
from jax import lax
from jax.experimental import pallas as pl
from jax.experimental.pallas import tpu as pltpu
from jax.sharding import PartitionSpec as P

MESH = pl.DeviceIdType.MESH
BF = jnp.bfloat16
F32 = jnp.float32

ROWS, D = 512, 1152
CH = 4
CROWS = ROWS // CH
HALF = D // 2
QROWS = HALF // 4
PARTS = 3
PCOLS = D // PARTS
TILES = (QROWS // 16) * (PCOLS // 128)
PIECE = -(-TILES // 4)
OWN, LEFT, RIGHT, PEER, PEER_LEFT, PEER_RIGHT, FAR = range(7)
TO_LEFT, TO_RIGHT, TO_PEER, FWD_LEFT, FWD_RIGHT, RELAY = range(6)

STRIDE = {"y": 32, "x": 8, "z": 2}
AXES = (
    (("y", "x", "z"), ("x", "y", "z"), ("y", "x", "z")),
    (("y", "x", "z"), ("x", "z", "y"), ("z", "y", "x")),
)


def dot(a, b, dims):
    return lax.dot_general(a, b, (dims, ((), ())), preferred_element_type=F32)


def kernel(
    scale_ref, bias_ref, ie_hbm, te_hbm, ip_hbm, tp_hbm,
    die_hbm, dte_hbm, dip_hbm, dtp_hbm,
    emb, proj, z, unit, inv, g, du, demb, dmat, half, r1, p2, r2, x3, a2, full,
    load_sem, out_sem, zs, zr, s0s, s0r, s1s, s1r, s2s, s2r, s3s, s3r, a2s, a2r, a1s, a1r, fs, fr,
):
    me = lax.axis_index("dp")
    core = lax.rem(me, 2)
    chip = lax.div(me, 2)
    at = {
        "z": lax.rem(chip, 4),
        "x": lax.rem(lax.div(chip, 4), 4),
        "y": lax.div(chip, 16),
    }
    peer = me + 1 - 2 * core
    left = lax.rem(me + 126, 128)
    right = lax.rem(me + 2, 128)
    relay_to = lax.rem(me + 127 + 2 * core, 128)

    def axis_peer(axis, d):
        return me + (lax.rem(at[axis] + d, 4) - at[axis]) * STRIDE[axis]

    loads = [
        pltpu.make_async_copy(te_hbm, emb.at[0], load_sem.at[0]),
        pltpu.make_async_copy(tp_hbm, proj.at[0], load_sem.at[1]),
        pltpu.make_async_copy(ie_hbm, emb.at[1], load_sem.at[2]),
        pltpu.make_async_copy(ip_hbm, proj.at[1], load_sem.at[3]),
    ]
    for load in loads:
        load.start()

    barrier = pltpu.get_barrier_semaphore()
    friends = [peer, left, right, relay_to]
    friends += [axis_peer(axis, d) for axis in ("z", "x", "y") for d in (1, 2, 3)]
    for friend in friends:
        pl.semaphore_signal(barrier, inc=1, device_id=(friend,), device_id_type=MESH)

    scale = jnp.exp(jnp.full((1, 1), scale_ref[0], F32))
    shift = jnp.full((1, 1), bias_ref[0], F32)

    started = []

    def send(src, dst, ssem, rsem, device):
        copy = pltpu.make_async_remote_copy(
            src_ref=src, dst_ref=dst, send_sem=ssem, recv_sem=rsem,
            device_id=(device,), device_id_type=MESH,
        )
        copy.start()
        started.append(copy)

    def await_recv(dst, rsem):
        pltpu.make_async_remote_copy(
            src_ref=dst, dst_ref=dst, send_sem=rsem, recv_sem=rsem,
            device_id=(peer,), device_id_type=MESH,
        ).wait_recv()

    def rows_of(c):
        return pl.ds(c * CROWS, CROWS)

    def send_block(side, src_slot, dst_slot, kind, c, device):
        send(
            z.at[side, src_slot, rows_of(c)], z.at[side, dst_slot, rows_of(c)],
            zs.at[side, kind, c], zr.at[side, dst_slot, c], device,
        )

    def await_block(side, slot, c):
        await_recv(z.at[side, slot, rows_of(c)], zr.at[side, slot, c])

    def make_unit(side):
        unit[side] = dot(emb[side], proj[side], ((1,), (0,)))

        def rows(i, _):
            at_rows = pl.ds(pl.multiple_of(i * 32, 32), 32)
            raw = unit[side, at_rows]
            over = 1.0 / jnp.sqrt(jnp.sum(raw * raw, axis=1, keepdims=True) + 1e-6)
            u = raw * over
            unit[side, at_rows] = u
            inv[side, at_rows] = over
            z[side, OWN, at_rows] = u.astype(BF)
            return 0

        lax.fori_loop(0, ROWS // 32, rows, 0)

    def send_own(side):
        for c in range(CH):
            send_block(side, OWN, RIGHT, TO_LEFT, c, left)
            send_block(side, OWN, LEFT, TO_RIGHT, c, right)
        for c in range(CH):
            send_block(side, OWN, PEER, TO_PEER, c, peer)

    def forward(side, c):
        await_block(side, LEFT, c)
        await_block(side, RIGHT, c)
        send_block(side, 2 - core, FAR, RELAY, c, relay_to)
        send_block(side, LEFT, PEER_LEFT, FWD_LEFT, c, peer)
        send_block(side, RIGHT, PEER_RIGHT, FWD_RIGHT, c, peer)

    def pair(side, slot, first, count, own=False, fresh=False):
        block = z[side, slot, pl.ds(first, count)]
        logits = scale * dot(z[1 - side, OWN], block, ((1,), (1,))) + shift
        coef = 1.0 / (1.0 + jnp.exp(-logits))
        if own:
            same = lax.broadcasted_iota(jnp.int32, coef.shape, 0) == (
                lax.broadcasted_iota(jnp.int32, coef.shape, 1) + first
            )
            coef = jnp.where(same, coef - 1.0, coef)
        term = dot(coef.astype(BF), block, ((1,), (0,)))
        g[...] = term if fresh else g[...] + term

    def halves(side, h):
        for slot in (LEFT, RIGHT, PEER_LEFT, PEER_RIGHT):
            if slot in (PEER_LEFT, PEER_RIGHT):
                for c in range(h * CH // 2, (h + 1) * CH // 2):
                    await_block(side, slot, c)
            pair(side, slot, h * ROWS // 2, ROWS // 2)

    def make_du(side):
        def rows(i, _):
            at_rows = pl.ds(pl.multiple_of(i * 32, 32), 32)
            grad = g[at_rows] * scale
            u = unit[side, at_rows]
            inner = jnp.sum(u * grad, axis=1, keepdims=True)
            du[side, at_rows] = ((grad - u * inner) * inv[side, at_rows]).astype(BF)
            return 0

        lax.fori_loop(0, ROWS // 32, rows, 0)

    def make_demb(side, out, sem):
        demb[side] = dot(du[side], proj[side], ((1,), (1,))).astype(BF)
        copy = pltpu.make_async_copy(demb.at[side], out, sem)
        copy.start()
        return copy

    def sum_steps(side, order):
        mine = pl.ds(pl.multiple_of(core * HALF, HALF), HALF)
        theirs = pl.ds(pl.multiple_of((1 - core) * HALF, HALF), HALF)
        cols = [pl.ds(p * PCOLS, PCOLS) for p in range(PARTS)]

        def quarter(i):
            return pl.ds(pl.multiple_of(i * QROWS, QROWS), QROWS)

        def own_rows(i):
            return pl.ds(pl.multiple_of(core * HALF + i * QROWS, QROWS), QROWS)

        def to_peer():
            for p in range(PARTS):
                dmat[side, :, cols[p]] = dot(
                    emb[side], du[side, :, cols[p]], ((0,), (0,))
                ).astype(BF)
                send(
                    dmat.at[side, theirs, cols[p]], half.at[side, :, cols[p]],
                    s0s.at[side, p], s0r.at[side, p], peer,
                )

        def first_axis():
            for p in range(PARTS):
                await_recv(half.at[side, :, cols[p]], s0r.at[side, p])
                half[side, :, cols[p]] = (
                    half[side, :, cols[p]].astype(F32) + dmat[side, mine, cols[p]].astype(F32)
                ).astype(BF)
                axis = order[p][0]
                for d in (1, 2, 3):
                    send(
                        half.at[side, quarter(lax.rem(at[axis] + d, 4)), cols[p]],
                        r1.at[side, p, d - 1],
                        s1s.at[side, p, d - 1], s1r.at[side, p, d - 1], axis_peer(axis, d),
                    )

        def second_axis():
            for p in range(PARTS):
                for d in range(3):
                    await_recv(r1.at[side, p, d], s1r.at[side, p, d])
                total = half[side, quarter(at[order[p][0]]), cols[p]].astype(F32)
                for d in range(3):
                    total = total + r1[side, p, d].astype(F32)
                total = total.astype(BF)
                for t in range(TILES):
                    r, c = divmod(t, PCOLS // 128)
                    p2[side, p, t // PIECE, pl.ds(t % PIECE * 16, 16)] = total[
                        r * 16 : r * 16 + 16, c * 128 : c * 128 + 128
                    ]
                for t in range(TILES, 4 * PIECE):
                    p2[side, p, t // PIECE, pl.ds(t % PIECE * 16, 16)] = jnp.zeros((16, 128), BF)
                axis = order[p][1]
                for d in (1, 2, 3):
                    send(
                        p2.at[side, p, lax.rem(at[axis] + d, 4)], r2.at[side, p, d - 1],
                        s2s.at[side, p, d - 1], s2r.at[side, p, d - 1], axis_peer(axis, d),
                    )

        def third_axis():
            for p in range(PARTS):
                for d in range(3):
                    await_recv(r2.at[side, p, d], s2r.at[side, p, d])
                total = p2[side, p, at[order[p][1]]].astype(F32)
                for d in range(3):
                    total = total + r2[side, p, d].astype(F32)
                axis = order[p][2]
                x3[side, p, at[axis]] = total.astype(BF)
                for d in (1, 2, 3):
                    send(
                        x3.at[side, p, at[axis]], x3.at[side, p, at[axis]],
                        s3s.at[side, p, d - 1], s3r.at[side, p, d - 1], axis_peer(axis, d),
                    )

        def second_back():
            for p in range(PARTS):
                axis = order[p][2]
                for d in (1, 2, 3):
                    await_recv(x3.at[side, p, lax.rem(at[axis] + 4 - d, 4)], s3r.at[side, p, d - 1])
                total = x3[side, p, 0].astype(F32)
                for i in (1, 2, 3):
                    total = total + x3[side, p, i].astype(F32)
                axis = order[p][1]
                a2[side, p, at[axis]] = total.astype(BF)
                for d in (1, 2, 3):
                    send(
                        a2.at[side, p, at[axis]], a2.at[side, p, at[axis]],
                        a2s.at[side, p, d - 1], a2r.at[side, p, d - 1], axis_peer(axis, d),
                    )

        def first_back():
            for p in range(PARTS):
                axis = order[p][1]
                for d in (1, 2, 3):
                    await_recv(a2.at[side, p, lax.rem(at[axis] + 4 - d, 4)], a2r.at[side, p, d - 1])
                axis = order[p][0]
                for t in range(TILES):
                    r, c = divmod(t, PCOLS // 128)
                    full[
                        side,
                        pl.ds(pl.multiple_of(core * HALF + at[axis] * QROWS + r * 16, 16), 16),
                        pl.ds(p * PCOLS + c * 128, 128),
                    ] = a2[side, p, t // PIECE, pl.ds(t % PIECE * 16, 16)]
                piece = full.at[side, own_rows(at[axis]), cols[p]]
                for d in (1, 2, 3):
                    send(piece, piece, a1s.at[side, p, d - 1], a1r.at[side, p, d - 1], axis_peer(axis, d))
                send(piece, piece, fs.at[side, p, 0], fr.at[side, p, 0], peer)

        def peer_back():
            for p in range(PARTS):
                axis = order[p][0]
                for d in (1, 2, 3):
                    piece = full.at[side, own_rows(lax.rem(at[axis] + 4 - d, 4)), cols[p]]
                    await_recv(piece, a1r.at[side, p, d - 1])
                    send(piece, piece, fs.at[side, p, d], fr.at[side, p, d], peer)

        def finish():
            for p in range(PARTS):
                axis = order[p][0]
                for d in range(4):
                    piece = full.at[
                        side,
                        pl.ds(
                            pl.multiple_of(
                                (1 - core) * HALF + lax.rem(at[axis] + 4 - d, 4) * QROWS, QROWS
                            ),
                            QROWS,
                        ),
                        cols[p],
                    ]
                    await_recv(piece, fr.at[side, p, d])

        return [
            to_peer, first_axis, second_axis, third_axis, second_back, first_back, peer_back, finish
        ]

    loads[0].wait()
    loads[1].wait()
    make_unit(0)
    pl.semaphore_wait(barrier, len(friends))
    send_own(0)
    loads[2].wait()
    loads[3].wait()
    make_unit(1)

    outs = []
    steps = []
    for side in (0, 1):
        def step():
            if steps:
                steps.pop(0)()

        for h in (0, 1):
            pair(side, OWN, h * ROWS // 2, ROWS // 2, own=True, fresh=h == 0)
        step()
        for c in range(CH):
            await_block(side, PEER, c)
        pair(side, PEER, 0, ROWS)
        step()
        for h in (0, 1):
            for c in range(h * CH // 2, (h + 1) * CH // 2):
                forward(side, c)
                step()
            if h == 1 and side == 0:
                send_own(1)
            halves(side, h)
            step()
        for c in range(CH):
            await_block(side, FAR, c)
        pair(side, FAR, 0, ROWS)
        while steps:
            step()
        target = 1 - side
        make_du(target)
        order = AXES[side]
        steps = sum_steps(target, order)
        steps.pop(0)()
        outs.append(make_demb(target, (die_hbm, dte_hbm)[side], out_sem.at[side]))
        if side == 1:
            outs.append(pltpu.make_async_copy(full.at[1], dip_hbm, out_sem.at[2]))
            outs[-1].start()
    while steps:
        steps.pop(0)()
    outs.append(pltpu.make_async_copy(full.at[0], dtp_hbm, out_sem.at[3]))
    outs[-1].start()
    for out in outs:
        out.wait()
    for copy in started:
        copy.wait_send()


def body(img_emb, txt_emb, img_proj, txt_proj, log_scale, bias):
    any_space = pl.BlockSpec(memory_space=pl.ANY)
    smem = pl.BlockSpec(memory_space=pltpu.SMEM)
    dma = pltpu.SemaphoreType.DMA
    d_img_emb, d_txt_emb, d_img_proj, d_txt_proj = pl.pallas_call(
        kernel,
        out_shape=(
            jax.ShapeDtypeStruct((ROWS, D), BF),
            jax.ShapeDtypeStruct((ROWS, D), BF),
            jax.ShapeDtypeStruct((D, D), BF),
            jax.ShapeDtypeStruct((D, D), BF),
        ),
        in_specs=[smem, smem] + [any_space] * 4,
        out_specs=(any_space,) * 4,
        scratch_shapes=[
            pltpu.VMEM((2, ROWS, D), BF),
            pltpu.VMEM((2, D, D), BF),
            pltpu.VMEM((2, 7, ROWS, D), BF),
            pltpu.VMEM((2, ROWS, D), F32),
            pltpu.VMEM((2, ROWS, 1), F32),
            pltpu.VMEM((ROWS, D), F32),
            pltpu.VMEM((2, ROWS, D), BF),
            pltpu.VMEM((2, ROWS, D), BF),
            pltpu.VMEM((2, D, D), BF),
            pltpu.VMEM((2, HALF, D), BF),
            pltpu.VMEM((2, PARTS, 3, QROWS, PCOLS), BF),
            pltpu.VMEM((2, PARTS, 4, PIECE * 16, 128), BF),
            pltpu.VMEM((2, PARTS, 3, PIECE * 16, 128), BF),
            pltpu.VMEM((2, PARTS, 4, PIECE * 16, 128), BF),
            pltpu.VMEM((2, PARTS, 4, PIECE * 16, 128), BF),
            pltpu.VMEM((2, D, D), BF),
            dma((4,)), dma((4,)),
            dma((2, 6, CH)), dma((2, 7, CH)),
            dma((2, PARTS)), dma((2, PARTS)),
            dma((2, PARTS, 3)), dma((2, PARTS, 3)),
            dma((2, PARTS, 3)), dma((2, PARTS, 3)),
            dma((2, PARTS, 3)), dma((2, PARTS, 3)),
            dma((2, PARTS, 3)), dma((2, PARTS, 3)),
            dma((2, PARTS, 3)), dma((2, PARTS, 3)),
            dma((2, PARTS, 4)), dma((2, PARTS, 4)),
        ],
        compiler_params=pltpu.CompilerParams(
            collective_id=0, has_side_effects=True, vmem_limit_bytes=62 << 20
        ),
        name="band_gradients",
    )(log_scale, bias, img_emb, txt_emb, img_proj, txt_proj)
    return (d_img_emb, d_txt_emb, d_img_proj.astype(F32), d_txt_proj.astype(F32))


def solution(mesh):
    return jax.shard_map(
        body,
        mesh=mesh,
        in_specs=(P("dp", None), P("dp", None), P(), P(), P(), P()),
        out_specs=(P("dp", None), P("dp", None), P(), P()),
        check_vma=False,
    )
```

time: 435 us -> 180 us (0.41)
  waiting for transfers between devices: 311 us -> 0 us
  Pallas kernels: 0 us -> 168 us
  starting transfers between devices: 48.2 us -> 0 us
  matrix products: 41.3 us -> 0 us
  between operations: 15.7 us -> 1.94 us
  local copies, waits for them, and re-layouts: 14.8 us -> 2.72 us
    pallas_call x0 -> x1, Pallas kernels: none -> 168 us  [body(): pl.pallas_call(kernel, out_shape=(jax.ShapeDtypeStruct((ROWS, D), BF), ja...]
    psum x1 -> x0, waiting for transfers between devices: 162 us -> none  [body(): lax.psum((img_weight_terms, txt_weight_terms), 'dp')]
    ppermute x14 -> x0, waiting for transfers between devices: 150 us -> none  [from_behind(): lax.ppermute(shard, axis, [(i, (i + by) % size) for i in range(size)])]
    ppermute x14 -> x0, starting transfers between devices: 48.2 us -> none  [from_behind(): lax.ppermute(shard, axis, [(i, (i + by) % size) for i in range(size)])]
    dot_general x27 -> x0, matrix products: 41.3 us -> none  [the longest x7 7.16 us: pair_grads(): jnp.dot(image_block, text_block.T, preferred_element_type=jnp.float32)]
    unnamed x16 -> x8, local copies, waits for them, and re-layouts: 14.8 us -> 2.72 us
    convert_element_type x9 -> x2, other arithmetic: 2.58 us -> 7.34 us  [the longest x1 4.62 us: body(): d_img_proj.astype(F32)]
  transfers between devices with their start and end apart: 15 -> 0, of which waited for: 15 -> 0; matrix products, arithmetic and copies ran while one was open for 8% -> 0% of each run, Pallas kernels for 0% -> 0%
where the time goes in v1:
time: 180 us
  Pallas kernels  168 us (93%)
  other arithmetic  7.34 us (4%)
  local copies, waits for them, and re-layouts  2.72 us (2%)
  between operations  1.94 us (1%)
    pallas_call x1, Pallas kernels, body(): pl.pallas_call(kernel, out_shape=(jax.ShapeDtypeStruct((ROWS, D), BF), ja...  168 us
    convert_element_type x1, other arithmetic, body(): d_img_proj.astype(F32)  4.62 us

profile of v1, /device:TPU:1, one launch (start us, length us, event | category | flops | bytes accessed | tf_op | source)
XLA Modules:
  0.0 180.1 jit_solution(635613832164262171)
XLA Ops:
  1.9 168.1 %band_gradients.1 = (bf16[512,1152]{1,0:T(8,128)(2,1)}, bf16[512,1152]{1,0:T(8,128)(2,1)}, bf16[1152,1152]{1,0:T(8,128)(2,1)}, bf16[1152,1152]{1,0:T(8,128)(2,1)}) custom-call(f32[1]{0:T(128)S(6)} %copy.12.scale_ref, f32[1]{0:T(128)S(6)} %copy.13.bias_ref, bf16[512,1152]{1,0:T(8,128)(2,1)} %ie_hbm.1, bf16[512,1152]{1,0:T(8,128)(2,1)} %te_hbm.1, ...), custom_call_target="tpu_custom_call" | custom-call | tf_op jit(solution)/shard_map/band_gradients/pallas_call | solution.py:363
  170.0 0.0 copy-start
  170.0 4.6 %convert_element_type.6 = f32[1152,1152]{1,0:T(8,128)} convert(bf16[1152,1152]{1,0:T(8,128)(2,1)} %get-tuple-element.10) | non-fusion elementwise | flops 1327104 | bytes 7962624 | tf_op jit(solution)/shard_map/convert_element_type | solution.py:405
  174.7 0.0 copy-done
  174.7 0.0 copy-start.2
  174.7 2.7 %convert_element_type.7 = f32[1152,1152]{1,0:T(8,128)} convert(bf16[1152,1152]{1,0:T(8,128)(2,1)S(1)} %copy-done) | non-fusion elementwise | flops 1327104 | bytes 7962624 | tf_op jit(solution)/shard_map/convert_element_type | solution.py:405
  177.4 0.0 copy-done.2
  177.4 0.0 copy-start.1
  177.4 1.0 copy.14
  178.4 0.7 copy-done.1
  179.1 1.0 copy.15
Async XLA Ops:
  170.0 4.6 %copy-start = (bf16[1152,1152]{1,0:T(8,128)(2,1)S(1)}, bf16[1152,1152]{1,0:T(8,128)(2,1)}, u32[]{:S(2)}) copy-start(bf16[1152,1152]{1,0:T(8,128)(2,1)} %get-tuple-element.11) | copy-start | bytes 7962628
  174.7 2.7 %copy-start.2 = (bf16[512,1152]{1,0:T(8,128)(2,1)S(1)}, bf16[512,1152]{1,0:T(8,128)(2,1)}, u32[]{:S(2)}) copy-start(bf16[512,1152]{1,0:T(8,128)(2,1)} %get-tuple-element.16) | copy-start | bytes 3538948
  177.4 1.7 copy-start.1

commit v2 on v1

--- a/solution.py
+++ b/solution.py
@@ -23,9 +23,11 @@
 OWN, LEFT, RIGHT, PEER, PEER_LEFT, PEER_RIGHT, FAR = range(7)
 TO_LEFT, TO_RIGHT, TO_PEER, FWD_LEFT, FWD_RIGHT, RELAY = range(6)
 
+STRIP = 128
+
 STRIDE = {"y": 32, "x": 8, "z": 2}
 AXES = (
-    (("y", "x", "z"), ("x", "y", "z"), ("y", "x", "z")),
+    (("y", "x", "z"), ("x", "z", "y"), ("z", "y", "x")),
     (("y", "x", "z"), ("x", "z", "y"), ("z", "y", "x")),
 )
 
@@ -62,7 +64,7 @@
         pltpu.make_async_copy(ie_hbm, emb.at[1], load_sem.at[2]),
         pltpu.make_async_copy(ip_hbm, proj.at[1], load_sem.at[3]),
     ]
-    for load in loads:
+    for load in loads[:2]:
         load.start()
 
     barrier = pltpu.get_barrier_semaphore()
@@ -102,27 +104,26 @@
     def await_block(side, slot, c):
         await_recv(z.at[side, slot, rows_of(c)], zr.at[side, slot, c])
 
-    def make_unit(side):
-        unit[side] = dot(emb[side], proj[side], ((1,), (0,)))
+    def make_unit(side, first=0, count=ROWS):
+        some = pl.ds(first, count)
+        unit[side, some] = dot(emb[side, some], proj[side], ((1,), (0,)))
 
         def rows(i, _):
-            at_rows = pl.ds(pl.multiple_of(i * 32, 32), 32)
+            at_rows = pl.ds(pl.multiple_of(first + i * STRIP, STRIP), STRIP)
             raw = unit[side, at_rows]
-            over = 1.0 / jnp.sqrt(jnp.sum(raw * raw, axis=1, keepdims=True) + 1e-6)
+            over = lax.rsqrt(jnp.sum(raw * raw, axis=1, keepdims=True) + 1e-6)
             u = raw * over
             unit[side, at_rows] = u
             inv[side, at_rows] = over
             z[side, OWN, at_rows] = u.astype(BF)
             return 0
 
-        lax.fori_loop(0, ROWS // 32, rows, 0)
-
-    def send_own(side):
-        for c in range(CH):
-            send_block(side, OWN, RIGHT, TO_LEFT, c, left)
-            send_block(side, OWN, LEFT, TO_RIGHT, c, right)
-        for c in range(CH):
-            send_block(side, OWN, PEER, TO_PEER, c, peer)
+        lax.fori_loop(0, count // STRIP, rows, 0)
+
+    def send_own(side, c):
+        send_block(side, OWN, RIGHT, TO_LEFT, c, left)
+        send_block(side, OWN, LEFT, TO_RIGHT, c, right)
+        send_block(side, OWN, PEER, TO_PEER, c, peer)
 
     def forward(side, c):
         await_block(side, LEFT, c)
@@ -152,14 +153,14 @@
 
     def make_du(side):
         def rows(i, _):
-            at_rows = pl.ds(pl.multiple_of(i * 32, 32), 32)
+            at_rows = pl.ds(pl.multiple_of(i * STRIP, STRIP), STRIP)
             grad = g[at_rows] * scale
             u = unit[side, at_rows]
             inner = jnp.sum(u * grad, axis=1, keepdims=True)
             du[side, at_rows] = ((grad - u * inner) * inv[side, at_rows]).astype(BF)
             return 0
 
-        lax.fori_loop(0, ROWS // 32, rows, 0)
+        lax.fori_loop(0, ROWS // STRIP, rows, 0)
 
     def make_demb(side, out, sem):
         demb[side] = dot(du[side], proj[side], ((1,), (1,))).astype(BF)
@@ -303,57 +304,119 @@
 
     loads[0].wait()
     loads[1].wait()
-    make_unit(0)
-    pl.semaphore_wait(barrier, len(friends))
-    send_own(0)
+    for load in loads[2:]:
+        load.start()
+    for h in (0, 1):
+        make_unit(0, h * ROWS // 2, ROWS // 2)
+        if h == 0:
+            pl.semaphore_wait(barrier, len(friends))
+        for c in range(h * CH // 2, (h + 1) * CH // 2):
+            send_own(0, c)
     loads[2].wait()
     loads[3].wait()
     make_unit(1)
 
-    outs = []
-    steps = []
-    for side in (0, 1):
-        def step():
-            if steps:
-                steps.pop(0)()
-
+    def finish_side(side):
+        target = 1 - side
+        make_du(target)
+        steps = sum_steps(target, AXES[side])
+        steps[0]()
+        return steps
+
+    def put_demb(side):
+        outs.append(make_demb(1 - side, (die_hbm, dte_hbm)[side], out_sem.at[side]))
+
+    def own_pair(side):
         for h in (0, 1):
             pair(side, OWN, h * ROWS // 2, ROWS // 2, own=True, fresh=h == 0)
-        step()
+
+    def peer_pair(side):
         for c in range(CH):
             await_block(side, PEER, c)
         pair(side, PEER, 0, ROWS)
-        step()
+
+    def far_pair(side):
         for h in (0, 1):
             for c in range(h * CH // 2, (h + 1) * CH // 2):
-                forward(side, c)
-                step()
-            if h == 1 and side == 0:
-                send_own(1)
-            halves(side, h)
-            step()
-        for c in range(CH):
-            await_block(side, FAR, c)
-        pair(side, FAR, 0, ROWS)
-        while steps:
-            step()
-        target = 1 - side
-        make_du(target)
-        order = AXES[side]
-        steps = sum_steps(target, order)
-        steps.pop(0)()
-        outs.append(make_demb(target, (die_hbm, dte_hbm)[side], out_sem.at[side]))
-        if side == 1:
-            outs.append(pltpu.make_async_copy(full.at[1], dip_hbm, out_sem.at[2]))
-            outs[-1].start()
-    while steps:
-        steps.pop(0)()
-    outs.append(pltpu.make_async_copy(full.at[0], dtp_hbm, out_sem.at[3]))
-    outs[-1].start()
+                await_block(side, FAR, c)
+            pair(side, FAR, h * ROWS // 2, ROWS // 2)
+
+    def put_out(target, out, sem):
+        outs.append(pltpu.make_async_copy(full.at[target], out, sem))
+        outs[-1].start()
+
+    outs = []
+    own_pair(0)
+    peer_pair(0)
+    forward(0, 0)
+    forward(0, 1)
+    halves(0, 0)
+    forward(0, 2)
+    forward(0, 3)
+    for c in range(CH):
+        send_own(1, c)
+    halves(0, 1)
+    far_pair(0)
+    image = finish_side(0)
+    own_pair(1)
+    peer_pair(1)
+    put_demb(0)
+    forward(1, 0)
+    forward(1, 1)
+    forward(1, 2)
+    forward(1, 3)
+    image[1]()
+    halves(1, 0)
+    halves(1, 1)
+    far_pair(1)
+    text = finish_side(1)
+    image[2]()
+    text[1]()
+    put_demb(1)
+    image[3]()
+    text[2]()
+    image[4]()
+    text[3]()
+    image[5]()
+    text[4]()
+    image[6]()
+    text[5]()
+    image[7]()
+    put_out(1, dip_hbm, out_sem.at[2])
+    text[6]()
+    text[7]()
+    put_out(0, dtp_hbm, out_sem.at[3])
     for out in outs:
         out.wait()
     for copy in started:
         copy.wait_send()
+
+
+def finish_kernel(ie, te, ip, tp, out_ie, out_te, out_ip, out_tp):
+    out_ie[...] = ie[...]
+    out_te[...] = te[...]
+    out_ip[...] = ip[...].astype(F32)
+    out_tp[...] = tp[...].astype(F32)
+
+
+def finish(*parts):
+    steps = 4
+
+    def spec(rows):
+        return pl.BlockSpec((rows // steps, D), lambda i: (i, 0))
+
+    specs = (spec(ROWS), spec(ROWS), spec(D), spec(D))
+    return pl.pallas_call(
+        finish_kernel,
+        grid=(steps,),
+        out_shape=tuple(
+            jax.ShapeDtypeStruct((n, D), kind) for n, kind in ((ROWS, BF), (ROWS, BF), (D, F32), (D, F32))
+        ),
+        in_specs=list(specs),
+        out_specs=specs,
+        compiler_params=pltpu.CompilerParams(vmem_limit_bytes=62 << 20),
+        name="finish",
+    )(*parts)
 
 
 def body(img_emb, txt_emb, img_proj, txt_proj, log_scale, bias):
@@ -402,7 +465,7 @@
         ),
         name="band_gradients",
     )(log_scale, bias, img_emb, txt_emb, img_proj, txt_proj)
-    return (d_img_emb, d_txt_emb, d_img_proj.astype(F32), d_txt_proj.astype(F32))
+    return finish(d_img_emb, d_txt_emb, d_img_proj, d_txt_proj)
 
 
 def solution(mesh):

time: 180 us -> 145 us (0.81)
  Pallas kernels: 168 us -> 143 us
  other arithmetic: 7.34 us -> 0 us
  local copies, waits for them, and re-layouts: 2.72 us -> 0 us
    pallas_call x1, Pallas kernels: 168 us -> 134 us  [body(): pl.pallas_call(kernel, out_shape=(jax.ShapeDtypeStruct((ROWS, D), BF), ja...]
    pallas_call x0 -> x1, Pallas kernels: none -> 8.49 us  [finish(): pl.pallas_call(finish_kernel, grid=(steps,), out_shape=tuple((jax.ShapeDt...]
    convert_element_type x2 -> x0, other arithmetic: 7.34 us -> none  [the longest x1 4.62 us: body(): d_img_proj.astype(F32)]
    unnamed x8 -> x0, local copies, waits for them, and re-layouts: 2.72 us -> none
where the time goes in v2:
time: 145 us; the launch traced here: 144 us
  Pallas kernels  143 us (99%)
  between operations  1.93 us (1%)
    pallas_call x1, Pallas kernels, body(): pl.pallas_call(kernel, out_shape=(jax.ShapeDtypeStruct((ROWS, D), BF), ja...  134 us
    pallas_call x1, Pallas kernels, finish(): pl.pallas_call(finish_kernel, grid=(steps,), out_shape=tuple((jax.ShapeDt...  8.49 us

profile of v2, /device:TPU:1, one launch (start us, length us, event | category | flops | bytes accessed | tf_op | source)
XLA Modules:
  0.0 144.5 jit_solution(13048723046789366596)
XLA Ops:
  1.9 134.1 %band_gradients.1 = (bf16[512,1152]{1,0:T(8,128)(2,1)}, bf16[512,1152]{1,0:T(8,128)(2,1)}, bf16[1152,1152]{1,0:T(8,128)(2,1)}, bf16[1152,1152]{1,0:T(8,128)(2,1)}) custom-call(f32[1]{0:T(128)S(6)} %copy.10.scale_ref, f32[1]{0:T(128)S(6)} %copy.11.bias_ref, bf16[512,1152]{1,0:T(8,128)(2,1)} %ie_hbm.1, bf16[512,1152]{1,0:T(8,128)(2,1)} %te_hbm.1, ...), custom_call_target="tpu_custom_call" | custom-call | tf_op jit(solution)/shard_map/band_gradients/pallas_call | solution.py:426
  136.0 8.5 %finish.1 = (bf16[512,1152]{1,0:T(8,128)(2,1)}, bf16[512,1152]{1,0:T(8,128)(2,1)}, f32[1152,1152]{1,0:T(8,128)}, f32[1152,1152]{1,0:T(8,128)}) custom-call(bf16[512,1152]{1,0:T(8,128)(2,1)} %get-tuple-element.8.ie, bf16[512,1152]{1,0:T(8,128)(2,1)} %get-tuple-element.9.te, bf16[1152,1152]{1,0:T(8,128)(2,1)} %get-tuple-element.10.ip, ...), custom_call_target="tpu_custom_call" | custom-call | tf_op jit(solution)/shard_map/finish/pallas_call | solution.py:409

commit v3 on v2

--- a/solution.py
+++ b/solution.py
@@ -24,6 +24,7 @@
 TO_LEFT, TO_RIGHT, TO_PEER, FWD_LEFT, FWD_RIGHT, RELAY = range(6)
 
 STRIP = 128
+PIECE_ROWS = 288
 
 STRIDE = {"y": 32, "x": 8, "z": 2}
 AXES = (
@@ -392,28 +393,55 @@
         copy.wait_send()
 
 
-def finish_kernel(ie, te, ip, tp, out_ie, out_te, out_ip, out_tp):
-    out_ie[...] = ie[...]
-    out_te[...] = te[...]
-    out_ip[...] = ip[...].astype(F32)
-    out_tp[...] = tp[...].astype(F32)
+def finish_kernel(ie, te, ip, tp, out_ie, out_te, out_ip, out_tp, narrow, wide, embs, sems):
+    emb_ins = [
+        pltpu.make_async_copy(src, embs.at[i], sems.at[2, i]) for i, src in enumerate((ie, te))
+    ]
+    emb_backs = [
+        pltpu.make_async_copy(embs.at[i], dst, sems.at[2, 2 + i])
+        for i, dst in enumerate((out_ie, out_te))
+    ]
+    pieces = [
+        (m, src, dst, pl.ds(c * PIECE_ROWS, PIECE_ROWS), c)
+        for c in range(D // PIECE_ROWS)
+        for m, (src, dst) in enumerate(((ip, out_ip), (tp, out_tp)))
+    ]
+    ins = [
+        pltpu.make_async_copy(src.at[rows], narrow.at[m, rows], sems.at[m, c])
+        for m, src, dst, rows, c in pieces
+    ]
+    backs = [
+        pltpu.make_async_copy(wide.at[m, rows], dst.at[rows], sems.at[3 + m, c])
+        for m, src, dst, rows, c in pieces
+    ]
+    for copy in ins + emb_ins:
+        copy.start()
+    for (m, src, dst, rows, c), copy, back in zip(pieces, ins, backs):
+        copy.wait()
+        wide[m, rows] = narrow[m, rows].astype(F32)
+        back.start()
+    for copy, back in zip(emb_ins, emb_backs):
+        copy.wait()
+        back.start()
+    for copy in backs + emb_backs:
+        copy.wait()
 
 
 def finish(*parts):
-    steps = 4
-
-    def spec(rows):
-        return pl.BlockSpec((rows // steps, D), lambda i: (i, 0))
-
-    specs = (spec(ROWS), spec(ROWS), spec(D), spec(D))
+    anywhere = pl.BlockSpec(memory_space=pl.ANY)
     return pl.pallas_call(
         finish_kernel,
-        grid=(steps,),
         out_shape=tuple(
             jax.ShapeDtypeStruct((n, D), kind) for n, kind in ((ROWS, BF), (ROWS, BF), (D, F32), (D, F32))
         ),
-        in_specs=list(specs),
-        out_specs=specs,
+        in_specs=[anywhere] * 4,
+        out_specs=(anywhere,) * 4,
+        scratch_shapes=[
+            pltpu.VMEM((2, D, D), BF),
+            pltpu.VMEM((2, D, D), F32),
+            pltpu.VMEM((2, ROWS, D), BF),
+            pltpu.SemaphoreType.DMA((5, D // PIECE_ROWS)),
+        ],
         compiler_params=pltpu.CompilerParams(vmem_limit_bytes=62 << 20),
         name="finish",
     )(*parts)

time: 145 us -> 143 us (0.986)
  Pallas kernels: 143 us -> 141 us
    pallas_call x1, Pallas kernels: 8.49 us -> 7.03 us  [finish(): pl.pallas_call(finish_kernel, out_shape=tuple((jax.ShapeDtypeStruct((n, D...]
where the time goes in v3:
time: 143 us
  Pallas kernels  141 us (99%)
  between operations  2.11 us (1%)
    pallas_call x1, Pallas kernels, body(): pl.pallas_call(kernel, out_shape=(jax.ShapeDtypeStruct((ROWS, D), BF), ja...  134 us
    pallas_call x1, Pallas kernels, finish(): pl.pallas_call(finish_kernel, out_shape=tuple((jax.ShapeDtypeStruct((n, D...  7.03 us

profile of v3, /device:TPU:1, one launch (start us, length us, event | category | flops | bytes accessed | tf_op | source)
XLA Modules:
  0.0 143.2 jit_solution(441061368709858636)
XLA Ops:
  1.9 134.1 %band_gradients.1 = (bf16[512,1152]{1,0:T(8,128)(2,1)}, bf16[512,1152]{1,0:T(8,128)(2,1)}, bf16[1152,1152]{1,0:T(8,128)(2,1)}, bf16[1152,1152]{1,0:T(8,128)(2,1)}) custom-call(f32[1]{0:T(128)S(6)} %copy.10.scale_ref, f32[1]{0:T(128)S(6)} %copy.11.bias_ref, bf16[512,1152]{1,0:T(8,128)(2,1)} %ie_hbm.1, bf16[512,1152]{1,0:T(8,128)(2,1)} %te_hbm.1, ...), custom_call_target="tpu_custom_call" | custom-call | tf_op jit(solution)/shard_map/band_gradients/pallas_call | solution.py:454
  136.0 7.0 %finish.1 = (bf16[512,1152]{1,0:T(8,128)(2,1)}, bf16[512,1152]{1,0:T(8,128)(2,1)}, f32[1152,1152]{1,0:T(8,128)}, f32[1152,1152]{1,0:T(8,128)}) custom-call(bf16[512,1152]{1,0:T(8,128)(2,1)} %get-tuple-element.8.ie, bf16[512,1152]{1,0:T(8,128)(2,1)} %get-tuple-element.9.te, bf16[1152,1152]{1,0:T(8,128)(2,1)} %get-tuple-element.10.ip, ...), custom_call_target="tpu_custom_call" | custom-call | tf_op jit(solution)/shard_map/finish/pallas_call | solution.py:432
